TPU v7x, 512 devices: a whole 4x4x16 slice. The times are simulated.
512 devices in a mesh: span: 32 (over z_lo, x), stream: 16 (over z_hi, y, core).
Axes of the slice: x: 4, y: 4, z: 16 (z_hi: 2, z_lo: 8; z = z_hi * 8 + z_lo), core: 2. Of those that a mesh axis runs over, the one named last changes fastest.
Arguments:
- divergence: bfloat16 [1536, 512, 256], P('span', 'stream'), may hold values from -6 to 6
- flow_basis: float32 [512, 512], P('stream'), may hold values from -1 to 2
- wall_basis: float32 [256, 256], replicated, may hold values from -1 to 2
- flow_mass: float32 [512], replicated, may hold values from 0.5 to 2
- wall_mass: float32 [256], replicated, may hold values from 0.5 to 2
- flow_eigen: float32 [512], replicated, may hold values from 0.2 to 2
- wall_eigen: float32 [256], replicated, may hold values from 0.2 to 2
Outputs:
- pressure: float32 [1536, 512, 256], P(('span', 'stream'))
All inputs are finite; a program needn't handle non-finite values.
Results may differ from a plain program's by a relative error of at most 0.0023.
Values may be sent and summed in bfloat16 or wider, within the bound.
A program may use at most 64 MiB of HBM per device.

v0:
```python
import math
import jax
import jax.numpy as jnp
from jax import lax
from jax.sharding import PartitionSpec as P


def fourier_rows(field_ids, length):
    midpoint = length // 2
    wavenum = jnp.where(field_ids <= midpoint, field_ids, field_ids - midpoint)
    planes = jnp.arange(length, dtype=jnp.int32)
    phase = wavenum[:, None] * planes[None, :] % length
    angle = phase.astype(jnp.float32) * jnp.float32(2.0 * math.pi / length)
    values = jnp.where((field_ids <= midpoint)[:, None], jnp.cos(angle), -jnp.sin(angle))
    return values.astype(jnp.bfloat16)


def wave_terms(field_ids, length):
    midpoint = length // 2
    wavenum = jnp.where(field_ids <= midpoint, field_ids, field_ids - midpoint).astype(jnp.float32)
    ratio = wavenum / jnp.float32(midpoint)
    return ratio * ratio


def local(divergence, flow_basis, wall_basis, flow_mass, wall_mass, flow_eigen, wall_eigen):
    highest = lax.Precision.HIGHEST
    span_count = lax.axis_size("span")
    flow_count = lax.axis_size("stream")
    plane_count, row_count, wall_count = divergence.shape
    field_count = plane_count * span_count
    owned_fields = plane_count // flow_count
    line_length = row_count * flow_count
    rows_order = jnp.arange(field_count, dtype=jnp.int32)
    table = fourier_rows(rows_order, field_count)
    slab_in = lax.all_to_all(divergence, "span", split_axis=1, concat_axis=0, tiled=True)
    flat = jnp.dot(table, slab_in.reshape(field_count, -1), preferred_element_type=jnp.float32)
    spectral = (flat * float(field_count) ** (-0.5)).reshape(
        field_count, slab_in.shape[1], slab_in.shape[2]
    )
    grouped = lax.all_to_all(spectral, "span", split_axis=0, concat_axis=1, tiled=True)
    lines = lax.all_to_all(grouped, "stream", split_axis=0, concat_axis=1, tiled=True)
    along_wall = jnp.dot(
        (lines * wall_mass[None, None, :]).reshape(-1, wall_count), wall_basis, precision=highest
    )
    weighted = along_wall.reshape(owned_fields, line_length, wall_count) * flow_mass[None, :, None]
    owned_ids = (
        lax.axis_index("span") * plane_count
        + lax.axis_index("stream") * owned_fields
        + jnp.arange(owned_fields, dtype=jnp.int32)
    )
    waves = wave_terms(owned_ids, field_count)
    denominator = flow_eigen[None, :, None] + wall_eigen[None, None, :] + waves[:, None, None]
    coeff = jnp.einsum(
        "xn,fxm->fnm",
        lax.all_gather(flow_basis, "stream", axis=0, tiled=True),
        weighted,
        precision=highest,
    )
    solved = coeff / denominator
    back = jnp.einsum(
        "xn,fnm->fxm",
        lax.all_gather(flow_basis, "stream", axis=0, tiled=True),
        solved,
        precision=highest,
    )
    pressure = jnp.dot(back.reshape(-1, wall_count), wall_basis.T, precision=highest)
    return pressure.reshape(owned_fields, line_length, wall_count)


def solution(mesh):
    return jax.shard_map(
        local,
        mesh=mesh,
        in_specs=(P("span", "stream", None), P("stream", None), P(), P(), P(), P(), P()),
        out_specs=P(("span", "stream"), None, None),
        check_vma=False,
    )
```

profile of v0, /device:TPU:1, one launch (start us, length us, event | category | flops | bytes accessed | tf_op | source)
XLA Modules:
  0.0 348.4 jit_solution(8871368069057873704)
XLA Ops:
  6.5 0.0 copy-start
  6.5 2.5 copy.22
  9.0 15.9 %all-to-all-start = ((bf16[48,32,256]{2,0,1:T(8,128)(2,1)}), bf16[48,32,256]{2,0,1:T(8,128)(2,1)S(1)}, u32[]{:S(2)}, u32[]{:S(2)}) async-start(bf16[48,32,256]{2,0,1:T(8,128)(2,1)} %copy.22), calls=%async_computation | async-start | bytes 1572864 | tf_op jit(solution)/shard_map/all_to_all | solution.py:35
  25.0 37.8 %all-to-all-done = bf16[48,32,256]{2,0,1:T(8,128)(2,1)S(1)} async-done(((bf16[48,32,256]{2,0,1:T(8,128)(2,1)}), bf16[48,32,256]{2,0,1:T(8,128)(2,1)S(1)}, u32[]{:S(2)}, u32[]{:S(2)}) %all-to-all-start) | async-done | bytes 786464 | tf_op jit(solution)/shard_map/all_to_all | solution.py:35
  62.8 52.7 %fusion.8 = f32[1536,1,256]{2,0,1:T(8,128)S(1)} fusion(bf16[1536,256]{1,0:T(8,128)(2,1)S(1)} %bitcast.39, s32[1536]{0:T(1024)S(1)} %add_select_fusion.1, pred[1536]{0:T(1024)(128)(4,1)S(1)} %iota_compare_fusion), kind=kOutput, calls=%fused_computation.11 | convolution fusion | flops 1236664320 | bytes 2366976 | tf_op jit(solution)/shard_map/dot_general | solution.py:36
  115.5 6.5 %copy.23 = f32[1536,1,256]{2,1,0:T(1,128)S(1)} copy(f32[1536,1,256]{2,0,1:T(8,128)S(1)} %fusion.8) | data formatting | bytes 3145728 | tf_op jit(solution)/shard_map/reshape | solution.py:37
  122.0 82.2 %all_to_all.51 = f32[1536,1,256]{2,1,0:T(1,128)S(1)} all-to-all(f32[1536,1,256]{2,1,0:T(1,128)S(1)} %copy.23), channel_id=1, replica_groups=mesh['span'=32,'stream'=16] {'span'}, dimensions={0} | all-to-all | bytes 3145728 | tf_op jit(solution)/shard_map/all_to_all | solution.py:40
  204.2 0.1 copy.30
  204.3 2.1 copy.24
  206.4 0.0 copy-start.2
  206.4 0.0 copy-start.4
  206.4 12.7 %all-to-all-start.2 = ((f32[48,32,256]{2,1,0:T(8,128)}), f32[48,32,256]{2,1,0:T(8,128)S(1)}, u32[]{:S(2)}, u32[]{:S(2)}) async-start(f32[48,32,256]{2,1,0:T(8,128)} %copy.24), calls=%async_computation.2 | async-start | bytes 3145728 | tf_op jit(solution)/shard_map/all_to_all | solution.py:41
  219.0 0.2 all-gather.2.cloned.1.call-start
  219.3 0.5 all-gather.2.cloned.1.call-update
  219.8 0.0 copy-done.2
  219.8 0.0 copy-done.4
  219.8 0.1 broadcast_add_fusion
  219.9 56.0 %all-to-all-done.2 = f32[48,32,256]{2,1,0:T(8,128)S(1)} async-done(((f32[48,32,256]{2,1,0:T(8,128)}), f32[48,32,256]{2,1,0:T(8,128)S(1)}, u32[]{:S(2)}, u32[]{:S(2)}) %all-to-all-start.2) | async-done | bytes 1572896 | tf_op jit(solution)/shard_map/all_to_all | solution.py:41
  275.9 0.0 copy-start.5
  275.9 0.2 copy.25
  276.1 0.5 copy-done.5
  276.6 0.1 bitcast_multiply_fusion
  276.8 0.0 copy-done
  276.8 0.0 copy-start.3
  276.8 1.4 fusion.21
  278.2 52.6 %all-gather.2.cloned.1.call-done = f32[512,512]{1,0:T(8,128)} async-done(((f32[32,512]{1,0:T(8,128)}), f32[512,512]{1,0:T(8,128)}) %all-gather.2.cloned.1.call-update) | async-done | bytes 1048592 | tf_op jit(solution)/shard_map/all_gather | solution.py:55
  330.8 0.0 copy-done.3
  330.8 0.0 copy-start.1
  330.8 4.1 %fusion.13 = f32[3,256,512]{2,1,0:T(8,128)S(1)} fusion(f32[3,512,256]{2,1,0:T(8,128)S(1)} %fusion.21, f32[512,512]{1,0:T(8,128)} %all-gather.2.cloned.1.call-done, f32[512]{0:T(512)S(1)} %copy-done.3), kind=kOutput, calls=%fused_computation.18 | convolution fusion | flops 2416312320 | bytes 4196352 | tf_op jit(solution)/shard_map/xn,fxm->fnm/dot_general | solution.py:53
  334.9 0.0 copy-done.1
  334.9 2.8 fusion.11
  337.7 3.9 %fusion.9 = f32[3,512,256]{2,1,0:T(8,128)} fusion(f32[3,256,512]{2,1,0:T(8,128)S(1)} %fusion.11, f32[256,256]{1,0:T(8,128)S(1)} %copy-done), kind=kOutput, calls=%fused_computation.12 | convolution fusion | flops 1207959552 | bytes 3407872 | tf_op jit(solution)/shard_map/dot_general | solution.py:66
  (3 shorter events, 0.0 us)
Async XLA Ops:
  6.5 270.2 %copy-start = (f32[256,256]{1,0:T(8,128)S(1)}, f32[256,256]{1,0:T(8,128)}, u32[]{:S(2)}) copy-start(f32[256,256]{1,0:T(8,128)} %param.9) | copy-start | bytes 786436
  9.0 53.7 %all-to-all-start = ((bf16[48,32,256]{2,0,1:T(8,128)(2,1)}), bf16[48,32,256]{2,0,1:T(8,128)(2,1)S(1)}, u32[]{:S(2)}, u32[]{:S(2)}) async-start(bf16[48,32,256]{2,0,1:T(8,128)(2,1)} %copy.22), calls=%async_computation | async-start | bytes 1572864 | tf_op jit(solution)/shard_map/all_to_all | solution.py:35
  206.4 13.4 %copy-start.2 = (f32[512]{0:T(512)S(1)}, f32[512]{0:T(512)}, u32[]{:S(2)}) copy-start(f32[512]{0:T(512)} %param.12) | copy-start | bytes 6148
  206.4 13.4 %copy-start.4 = (f32[256]{0:T(256)S(1)}, f32[256]{0:T(256)}, u32[]{:S(2)}) copy-start(f32[256]{0:T(256)} %param.13) | copy-start | bytes 3076
  206.4 69.6 %all-to-all-start.2 = ((f32[48,32,256]{2,1,0:T(8,128)}), f32[48,32,256]{2,1,0:T(8,128)S(1)}, u32[]{:S(2)}, u32[]{:S(2)}) async-start(f32[48,32,256]{2,1,0:T(8,128)} %copy.24), calls=%async_computation.2 | async-start | bytes 3145728 | tf_op jit(solution)/shard_map/all_to_all | solution.py:41
  219.0 111.8 %all-gather.2.cloned.1.call-start = ((), (), s32[]{:S(2)}) async-start(), calls=%async_computation.3 | async-start | bytes 1114112 | tf_op jit(solution)/shard_map/all_gather | solution.py:55
  275.9 0.7 copy-start.5
  276.8 54.0 %copy-start.3 = (f32[512]{0:T(512)S(1)}, f32[512]{0:T(512)}, u32[]{:S(2)}) copy-start(f32[512]{0:T(512)} %param.10) | copy-start | bytes 6148
  330.8 4.1 %copy-start.1 = (f32[512,512]{1,0:T(8,128)S(1)}, f32[512,512]{1,0:T(8,128)}, u32[]{:S(2)}) copy-start(f32[512,512]{1,0:T(8,128)} %all-gather.2.cloned.1.call-done) | copy-start | bytes 3145732
Sparse Core Ops, SparseCore 0:
  223.2 107.5 all-gather.1
where the time goes:
time: 349 us; the launch traced here: 348 us
  waiting for transfers between devices  147 us (42%)
  blocking collectives  82.2 us (24%)
  matrix products  64.8 us (19%)
  starting transfers between devices  28.8 us (8%)
  between operations  13.5 us (4%)
  local copies, waits for them, and re-layouts  11.8 us (3%)
    all_to_all x1, blocking collectives, local(): lax.all_to_all(spectral, 'span', split_axis=0, concat_axis=1, tiled=True)  82.2 us
    all_to_all x1, waiting for transfers between devices, local(): lax.all_to_all(grouped, 'stream', split_axis=0, concat_axis=1, tiled=True)  56 us
    dot_general x1, matrix products, local(): jnp.dot(table, slab_in.reshape(field_count, -1), preferred_element_type=j...  52.7 us
    all_gather x1, waiting for transfers between devices, local(): lax.all_gather(flow_basis, 'stream', axis=0, tiled=True)  52.6 us
    all_to_all x1, waiting for transfers between devices, local(): lax.all_to_all(divergence, 'span', split_axis=1, concat_axis=0, tiled=True)  37.8 us
    all_to_all x1, starting transfers between devices, local(): lax.all_to_all(divergence, 'span', split_axis=1, concat_axis=0, tiled=True)  15.9 us
    all_to_all x1, starting transfers between devices, local(): lax.all_to_all(grouped, 'stream', split_axis=0, concat_axis=1, tiled=True)  12.7 us
  transfers between devices with their start and end apart: 3, of which 3 were waited for; matrix products, arithmetic and copies ran while one was open for 1% of the time, Pallas kernels for 0%

commit v1 on v0

--- a/solution.py
+++ b/solution.py
@@ -3,6 +3,11 @@
 import jax.numpy as jnp
 from jax import lax
 from jax.sharding import PartitionSpec as P
+
+
+def all_by_exchange(array, axis, dim):
+    sent = jnp.stack([array] * lax.axis_size(axis))
+    return jnp.concatenate(lax.all_to_all(sent, axis, 0, 0), axis=dim)
 
 
 def fourier_rows(field_ids, length):
@@ -51,10 +56,7 @@
     waves = wave_terms(owned_ids, field_count)
     denominator = flow_eigen[None, :, None] + wall_eigen[None, None, :] + waves[:, None, None]
     coeff = jnp.einsum(
-        "xn,fxm->fnm",
-        lax.all_gather(flow_basis, "stream", axis=0, tiled=True),
-        weighted,
-        precision=highest,
+        "xn,fxm->fnm", all_by_exchange(flow_basis, "stream", 0), weighted, precision=highest
     )
     solved = coeff / denominator
     back = jnp.einsum(

time: 349 us -> 421 us (1.21)
  blocking collectives: 82.2 us -> 151 us
  starting transfers between devices: 28.8 us -> 43.7 us
  waiting for transfers between devices: 147 us -> 133 us
    all_to_all x0 -> x1, blocking collectives: none -> 68.8 us  [local(): lax.all_to_all(grouped, 'stream', split_axis=0, concat_axis=1, tiled=True)]
    all_to_all x1, starting transfers between devices: 12.7 us -> 27.6 us  [all_by_exchange(): return jnp.concatenate(lax.all_to_all(sent, axis, 0, 0), axis=dim)]
    all_to_all x1, waiting for transfers between devices: 56 us -> 41.4 us  [all_by_exchange(): return jnp.concatenate(lax.all_to_all(sent, axis, 0, 0), axis=dim)]
where the time goes in v1:
time: 421 us; the launch traced here: 420 us
  blocking collectives  151 us (36%)
  waiting for transfers between devices  133 us (32%)
  matrix products  66.4 us (16%)
  starting transfers between devices  43.7 us (10%)
  between operations  13.6 us (3%)
  local copies, waits for them, and re-layouts  11.8 us (3%)
    all_to_all x1, blocking collectives, local(): lax.all_to_all(spectral, 'span', split_axis=0, concat_axis=1, tiled=True)  82.2 us
    all_to_all x1, blocking collectives, local(): lax.all_to_all(grouped, 'stream', split_axis=0, concat_axis=1, tiled=True)  68.8 us
    all_gather x1, waiting for transfers between devices, local(): lax.all_gather(flow_basis, 'stream', axis=0, tiled=True)  53.7 us
    dot_general x1, matrix products, local(): jnp.dot(table, slab_in.reshape(field_count, -1), preferred_element_type=j...  52.7 us
    all_to_all x1, waiting for transfers between devices, all_by_exchange(): return jnp.concatenate(lax.all_to_all(sent, axis, 0, 0), axis=dim)  41.4 us
    all_to_all x1, waiting for transfers between devices, local(): lax.all_to_all(divergence, 'span', split_axis=1, concat_axis=0, tiled=True)  37.8 us
    all_to_all x1, starting transfers between devices, all_by_exchange(): return jnp.concatenate(lax.all_to_all(sent, axis, 0, 0), axis=dim)  27.6 us
    all_to_all x1, starting transfers between devices, local(): lax.all_to_all(divergence, 'span', split_axis=1, concat_axis=0, tiled=True)  15.9 us
  transfers between devices with their start and end apart: 3, of which 3 were waited for; matrix products, arithmetic and copies ran while one was open for 1% of the time, Pallas kernels for 0%

profile of v1, /device:TPU:1, one launch (start us, length us, event | category | flops | bytes accessed | tf_op | source)
XLA Modules:
  0.0 420.1 jit_solution(7604329062800715749)
XLA Ops:
  6.5 0.0 copy-start
  6.5 2.5 copy.22
  9.0 15.9 %all-to-all-start = ((bf16[48,32,256]{2,0,1:T(8,128)(2,1)}), bf16[48,32,256]{2,0,1:T(8,128)(2,1)S(1)}, u32[]{:S(2)}, u32[]{:S(2)}) async-start(bf16[48,32,256]{2,0,1:T(8,128)(2,1)} %copy.22), calls=%async_computation | async-start | bytes 1572864 | tf_op jit(solution)/shard_map/all_to_all | solution.py:40
  25.0 37.8 %all-to-all-done = bf16[48,32,256]{2,0,1:T(8,128)(2,1)S(1)} async-done(((bf16[48,32,256]{2,0,1:T(8,128)(2,1)}), bf16[48,32,256]{2,0,1:T(8,128)(2,1)S(1)}, u32[]{:S(2)}, u32[]{:S(2)}) %all-to-all-start) | async-done | bytes 786464 | tf_op jit(solution)/shard_map/all_to_all | solution.py:40
  62.8 52.7 %fusion.8 = f32[1536,1,256]{2,0,1:T(8,128)S(1)} fusion(bf16[1536,256]{1,0:T(8,128)(2,1)S(1)} %bitcast.42, s32[1536]{0:T(1024)S(1)} %add_select_fusion.1, pred[1536]{0:T(1024)(128)(4,1)S(1)} %iota_compare_fusion), kind=kOutput, calls=%fused_computation.11 | convolution fusion | flops 1236664320 | bytes 2366976 | tf_op jit(solution)/shard_map/dot_general | solution.py:41
  115.5 6.5 %copy.23 = f32[1536,1,256]{2,1,0:T(1,128)S(1)} copy(f32[1536,1,256]{2,0,1:T(8,128)S(1)} %fusion.8) | data formatting | bytes 3145728 | tf_op jit(solution)/shard_map/reshape | solution.py:42
  122.0 82.2 %all_to_all.56 = f32[1536,1,256]{2,1,0:T(1,128)S(1)} all-to-all(f32[1536,1,256]{2,1,0:T(1,128)S(1)} %copy.23), channel_id=1, replica_groups=mesh['span'=32,'stream'=16] {'span'}, dimensions={0} | all-to-all | bytes 3145728 | tf_op jit(solution)/shard_map/all_to_all | solution.py:45
  204.2 0.1 copy.30
  204.3 0.9 copy.24
  205.2 0.0 copy-start.1
  205.2 68.8 %all_to_all.57 = f32[48,32,256]{2,1,0:T(8,128)S(1)} all-to-all(f32[48,32,256]{2,1,0:T(8,128)S(1)} %copy.24), channel_id=1, replica_groups=mesh['span'=32,'stream'=16] {'stream'}, dimensions={0} | all-to-all | bytes 3145728 | tf_op jit(solution)/shard_map/all_to_all | solution.py:46
  274.1 0.0 copy-done.1
  274.1 0.0 copy-start.2
  274.1 0.0 copy-start.4
  274.1 1.1 stack.2
  275.2 27.6 %all-to-all-start.3 = ((f32[16,32,512]{2,1,0:T(8,128)}), f32[16,32,512]{2,1,0:T(8,128)S(1)}, u32[]{:S(2)}, u32[]{:S(2)}) async-start(f32[16,32,512]{2,1,0:T(8,128)} %stack.2), calls=%async_computation.3 | async-start | bytes 2097152 | tf_op jit(solution)/shard_map/all_to_all | solution.py:10
  302.8 0.2 all-gather.2.cloned.1.call-start
  303.0 0.5 all-gather.2.cloned.1.call-update
  303.5 0.0 copy-done.2
  303.5 0.0 copy-done.4
  303.5 0.1 broadcast_add_fusion
  303.6 0.0 copy-start.5
  303.7 0.2 copy.25
  303.8 0.5 copy-done.5
  304.3 0.1 bitcast_multiply_fusion
  304.5 0.0 copy-done
  304.5 0.0 copy-start.3
  304.5 1.4 fusion.20
  305.9 41.4 %all-to-all-done.3 = f32[16,32,512]{2,1,0:T(8,128)S(1)} async-done(((f32[16,32,512]{2,1,0:T(8,128)}), f32[16,32,512]{2,1,0:T(8,128)S(1)}, u32[]{:S(2)}, u32[]{:S(2)}) %all-to-all-start.3) | async-done | bytes 1048608 | tf_op jit(solution)/shard_map/all_to_all | solution.py:10
  347.3 0.0 copy-done.3
  347.3 3.9 fusion.13
  351.2 53.7 %all-gather.2.cloned.1.call-done = f32[512,512]{1,0:T(8,128)} async-done(((f32[32,512]{1,0:T(8,128)}), f32[512,512]{1,0:T(8,128)}) %all-gather.2.cloned.1.call-update) | async-done | bytes 1048592 | tf_op jit(solution)/shard_map/all_gather | solution.py:64
  404.9 4.5 %fusion.11 = f32[3,256,512]{2,1,0:T(8,128)S(1)} fusion(f32[3,256,512]{2,1,0:T(8,128)} %fusion.13, f32[512,512]{1,0:T(8,128)} %all-gather.2.cloned.1.call-done, f32[3]{0:T(128)S(1)} %fusion.24, f32[512,256]{0,1:T(8,128)S(1)} %broadcast_add_fusion), kind=kOutput, calls=%fused_computation.15 | convolution fusion | flops 2416705536 | bytes 4718604 | tf_op jit(solution)/shard_map/xn,fnm->fxm/dot_general | solution.py:62
  409.4 3.9 fusion.9
  (3 shorter events, 0.0 us)
Async XLA Ops:
  6.5 297.9 %copy-start = (f32[256,256]{1,0:T(8,128)S(1)}, f32[256,256]{1,0:T(8,128)}, u32[]{:S(2)}) copy-start(f32[256,256]{1,0:T(8,128)} %param.9) | copy-start | bytes 786436
  9.0 53.7 %all-to-all-start = ((bf16[48,32,256]{2,0,1:T(8,128)(2,1)}), bf16[48,32,256]{2,0,1:T(8,128)(2,1)S(1)}, u32[]{:S(2)}, u32[]{:S(2)}) async-start(bf16[48,32,256]{2,0,1:T(8,128)(2,1)} %copy.22), calls=%async_computation | async-start | bytes 1572864 | tf_op jit(solution)/shard_map/all_to_all | solution.py:40
  205.2 68.8 %copy-start.1 = (f32[32,512]{1,0:T(8,128)S(1)}, f32[32,512]{1,0:T(8,128)}, u32[]{:S(2)}) copy-start(f32[32,512]{1,0:T(8,128)} %param.8) | copy-start | bytes 196612
  274.1 29.5 %copy-start.2 = (f32[512]{0:T(512)S(1)}, f32[512]{0:T(512)}, u32[]{:S(2)}) copy-start(f32[512]{0:T(512)} %param.12) | copy-start | bytes 6148
  274.1 29.5 %copy-start.4 = (f32[256]{0:T(256)S(1)}, f32[256]{0:T(256)}, u32[]{:S(2)}) copy-start(f32[256]{0:T(256)} %param.13) | copy-start | bytes 3076
  275.2 72.2 %all-to-all-start.3 = ((f32[16,32,512]{2,1,0:T(8,128)}), f32[16,32,512]{2,1,0:T(8,128)S(1)}, u32[]{:S(2)}, u32[]{:S(2)}) async-start(f32[16,32,512]{2,1,0:T(8,128)} %stack.2), calls=%async_computation.3 | async-start | bytes 2097152 | tf_op jit(solution)/shard_map/all_to_all | solution.py:10
  302.8 102.2 %all-gather.2.cloned.1.call-start = ((), (), s32[]{:S(2)}) async-start(), calls=%async_computation.4 | async-start | bytes 1114112 | tf_op jit(solution)/shard_map/all_gather | solution.py:64
  303.6 0.7 copy-start.5
  304.5 42.8 %copy-start.3 = (f32[512]{0:T(512)S(1)}, f32[512]{0:T(512)}, u32[]{:S(2)}) copy-start(f32[512]{0:T(512)} %param.10) | copy-start | bytes 6148
Sparse Core Ops, SparseCore 0:
  306.9 97.9 all-gather.1
